TPU v7x, 32 devices: a whole 2x2x4 slice. The times are simulated.
32 devices in a mesh: groups: 2 (over y), expert: 4 (over z), dp: 4 (over x, core).
Axes of the slice: x: 2, y: 2, z: 4, core: 2. Of those that a mesh axis runs over, the one named last changes fastest.
Arguments:
- tokens: bfloat16 [32, 256, 1280], P(('groups', 'expert', 'dp')), parts along dimension 0, may hold values from -8 to 8
- cotangent: bfloat16 [32, 256, 1280], P(('groups', 'expert', 'dp')), parts along dimension 0, may hold values from -6 to 6
- slot_params: bfloat16 [1280, 8], replicated, may hold values from -4 to 4
- inner_weight: bfloat16 [4, 1280, 4096], P('expert', None, 'dp'), may hold values from -0.15625 to 0.15625
- outer_weight: bfloat16 [4, 4096, 1280], P('expert', 'dp'), may hold values from -0.09375 to 0.09375
Outputs:
- grad_tokens: bfloat16 [32, 256, 1280], P(('groups', 'expert', 'dp')), parts along dimension 0
- grad_slot_params: float32 [2560, 8], P('groups'), parts along dimension 0
- grad_inner: bfloat16 [8, 1280, 4096], P(('groups', 'expert'), None, 'dp'), parts along dimension 0
- grad_outer: bfloat16 [8, 4096, 1280], P(('groups', 'expert'), 'dp'), parts along dimension 0
There are 2 independent parts, one for each index of `groups`. A program takes and returns all parts, laid end to end along the dimension named above; an argument that names none is the same for every part. Nothing has to cross between parts.
All inputs are finite; a program needn't handle non-finite values.
Results may differ from a plain program's by a relative error of at most 0.02.
Values may be sent and summed in bfloat16 or wider, within the bound.
A program may use at most 64 MiB of HBM per device.

v0:
```python
import jax
import jax.numpy as jnp
from jax import lax
from jax.sharding import PartitionSpec as P


def gelu_tanh(values):
    return jax.nn.gelu(values, approximate=True)


def local(tokens, cotangent, slot_params, inner_weight, outer_weight):
    images = tokens.shape[0]
    model_width = tokens.shape[2]
    columns = slot_params.shape[1]
    experts = lax.axis_size("expert")
    slot_count = columns // experts
    first_proj = inner_weight[0]
    second_proj = outer_weight[0]
    logits = jnp.einsum("itd,dc->ict", tokens, slot_params, preferred_element_type=jnp.float32)
    dispatch_exact = jax.nn.softmax(logits, axis=2)
    combine_exact = jax.nn.softmax(logits, axis=1)
    dispatch = dispatch_exact.astype(jnp.bfloat16)
    combine = combine_exact.astype(jnp.bfloat16)
    slot_in = jnp.einsum(
        "ict,itd->icd", dispatch, tokens, preferred_element_type=jnp.float32
    ).astype(jnp.bfloat16)
    slot_in = slot_in.reshape(images, experts, slot_count, model_width)
    arrived = lax.all_to_all(slot_in, "expert", split_axis=1, concat_axis=1, tiled=True)
    preact = jnp.einsum(
        "nesd,df->nesf",
        lax.all_gather(arrived, "dp", axis=0, tiled=True),
        first_proj,
        preferred_element_type=jnp.float32,
    )
    hidden = gelu_tanh(preact).astype(jnp.bfloat16)
    rows_part = hidden
    summed = lax.psum_scatter(
        jnp.einsum(
            "nesf,fd->nesd", rows_part, second_proj, preferred_element_type=jnp.float32
        ).astype(jnp.bfloat16),
        "dp",
        scatter_dimension=0,
        tiled=True,
    )
    slot_out = lax.all_to_all(summed, "expert", split_axis=1, concat_axis=1, tiled=True).reshape(
        images, columns, model_width
    )
    g_slot_out = jnp.einsum(
        "ict,itd->icd", combine, cotangent, preferred_element_type=jnp.float32
    ).astype(jnp.bfloat16)
    g_combine = jnp.einsum("itd,icd->ict", cotangent, slot_out, preferred_element_type=jnp.float32)
    g_logit_combine = combine_exact * (
        g_combine - jnp.sum(combine_exact * g_combine, axis=1, keepdims=True)
    )
    sent_grads = lax.all_to_all(
        g_slot_out.reshape(images, experts, slot_count, model_width),
        "expert",
        split_axis=1,
        concat_axis=1,
        tiled=True,
    )
    shard_piece = lax.all_gather(sent_grads, "dp", axis=0, tiled=True)
    outer_acc = jnp.einsum("nesf,nesd->fd", hidden, shard_piece, preferred_element_type=jnp.float32)
    g_hidden_part = jnp.einsum(
        "nesd,fd->nesf", shard_piece, second_proj, preferred_element_type=jnp.float32
    )
    outer_acc, g_hidden = (outer_acc, g_hidden_part)
    unused, pull = jax.vjp(gelu_tanh, preact)
    g_preact = pull(g_hidden)[0].astype(jnp.bfloat16)
    inner_acc = jnp.einsum(
        "nesd,nesf->df",
        lax.all_gather(arrived, "dp", axis=0, tiled=True),
        g_preact,
        preferred_element_type=jnp.float32,
    )
    rows_part = g_preact
    g_back = lax.psum_scatter(
        jnp.einsum(
            "nesf,df->nesd", rows_part, first_proj, preferred_element_type=jnp.float32
        ).astype(jnp.bfloat16),
        "dp",
        scatter_dimension=0,
        tiled=True,
    )
    g_slot_in = lax.all_to_all(g_back, "expert", split_axis=1, concat_axis=1, tiled=True).reshape(
        images, columns, model_width
    )
    g_dispatch = jnp.einsum("itd,icd->ict", tokens, g_slot_in, preferred_element_type=jnp.float32)
    g_logit_dispatch = dispatch_exact * (
        g_dispatch - jnp.sum(dispatch_exact * g_dispatch, axis=2, keepdims=True)
    )
    g_logits = (g_logit_combine + g_logit_dispatch).astype(jnp.bfloat16)
    token_grad = jnp.einsum("ict,icd->itd", dispatch, g_slot_in, preferred_element_type=jnp.float32)
    token_grad = token_grad + jnp.einsum(
        "ict,dc->itd", g_logits, slot_params, preferred_element_type=jnp.float32
    )
    local_params = jnp.einsum("itd,ict->dc", tokens, g_logits, preferred_element_type=jnp.float32)
    params_grad = lax.psum(local_params, ("expert", "dp"))
    return (
        token_grad.astype(jnp.bfloat16),
        params_grad,
        inner_acc[None].astype(jnp.bfloat16),
        outer_acc[None].astype(jnp.bfloat16),
    )


def solution(mesh):
    return jax.shard_map(
        local,
        mesh=mesh,
        in_specs=(
            P(("groups", "expert", "dp"), None, None),
            P(("groups", "expert", "dp"), None, None),
            P(),
            P("expert", None, "dp"),
            P("expert", "dp", None),
        ),
        out_specs=(
            P(("groups", "expert", "dp"), None, None),
            P("groups", None),
            P(("groups", "expert"), None, "dp"),
            P(("groups", "expert"), "dp", None),
        ),
        check_vma=False,
    )
```

profile of v0, /device:TPU:0, one launch (start us, length us, event | category | flops | bytes accessed | tf_op | source)
XLA Modules:
  0.0 169.2 jit_solution(16960794477839923736)
XLA Ops:
  7.2 0.0 copy-start
  7.2 1.7 fusion.47
  8.9 0.2 fusion.39
  9.1 1.3 convolution_convert_fusion
  10.4 0.6 reshape.111
  11.0 6.3 %all-to-all-start.1 = ((bf16[1,4,2,1280]{3,2,0,1:T(2,128)(2,1)}), bf16[1,4,2,1280]{3,2,0,1:T(2,128)(2,1)S(1)}, u32[]{:S(2)}, u32[]{:S(2)}) async-start(bf16[1,4,2,1280]{3,2,0,1:T(2,128)(2,1)} %bitcast.6), calls=%async_computation.1 | async-start | bytes 40960 | tf_op jit(solution)/shard_map/all_to_all | solution.py:28
  17.4 1.3 convolution_convert_fusion.1
  18.6 0.6 reshape.110
  19.3 1.3 dynamic-slice
  20.6 2.4 %all-to-all-done.1 = bf16[1,4,2,1280]{3,2,0,1:T(2,128)(2,1)S(1)} async-done(((bf16[1,4,2,1280]{3,2,0,1:T(2,128)(2,1)}), bf16[1,4,2,1280]{3,2,0,1:T(2,128)(2,1)S(1)}, u32[]{:S(2)}, u32[]{:S(2)}) %all-to-all-start.1) | async-done | bytes 20512 | tf_op jit(solution)/shard_map/all_to_all | solution.py:28
  23.0 3.3 %all-to-all-start = ((bf16[1,4,2,1280]{3,2,0,1:T(2,128)(2,1)}), bf16[1,4,2,1280]{3,2,0,1:T(2,128)(2,1)S(1)}, u32[]{:S(2)}, u32[]{:S(2)}) async-start(bf16[1,4,2,1280]{3,2,0,1:T(2,128)(2,1)} %bitcast.2), calls=%async_computation | async-start | bytes 40960 | tf_op jit(solution)/shard_map/all_to_all | solution.py:55
  26.2 0.0 all-reduce.5.cloned.1.call-start
  26.3 5.3 %all_gather.8 = bf16[4,4,2,1280]{3,1,2,0:T(4,128)(2,1)S(1)} all-gather(bf16[1,4,2,1280]{3,1,2,0:T(4,128)(2,1)S(1)} %copy.26), channel_id=1, replica_groups=mesh['groups'=2,'expert'=4,'dp'=4] {'dp'}, dimensions={0}, use_global_device_ids=true | all-gather | bytes 102400 | tf_op jit(solution)/shard_map/all_gather | solution.py:31
  31.6 0.2 all-to-all-done
  31.9 5.3 %all_gather.7 = bf16[4,4,2,1280]{3,1,2,0:T(4,128)(2,1)S(1)} all-gather(bf16[1,4,2,1280]{3,1,2,0:T(4,128)(2,1)S(1)} %copy.24), channel_id=1, replica_groups=mesh['groups'=2,'expert'=4,'dp'=4] {'dp'}, dimensions={0}, use_global_device_ids=true | all-gather | bytes 102400 | tf_op jit(solution)/shard_map/all_gather | solution.py:62
  37.1 2.3 %fusion.4 = f32[4,4,2,1024]{3,1,2,0:T(4,128)S(1)} fusion(bf16[4,4,2,1280]{3,1,2,0:T(4,128)(2,1)S(1)} %all_gather.8, bf16[1,1280,1024]{2,1,0:T(8,128)(2,1)} %param.8), kind=kOutput, calls=%fused_computation.7 | convolution fusion | flops 83886080 | bytes 2834432 | tf_op jit(solution)/shard_map/nesd,df->nesf/dot_general | solution.py:29
  39.4 0.0 copy-done
  39.4 1.2 fusion.12
  40.6 0.9 fusion.33
  41.6 0.0 copy-start.1
  41.6 2.4 %fusion.1 = bf16[1,1024,1280]{2,1,0:T(8,128)(2,1)} fusion(bf16[4,4,2,1280]{3,1,2,0:T(4,128)(2,1)S(1)} %all_gather.7, f32[4,4,2,1024]{3,1,2,0:T(4,128)S(1)} %fusion.4), kind=kOutput, calls=%fused_computation.3 | convolution fusion | flops 85491712 | bytes 2834432 | tf_op jit(solution)/shard_map/nesf,nesd->fd/dot_general | solution.py:63
  44.0 0.0 copy-done.1
  44.0 1.5 fusion.15
  45.6 0.0 all-reduce.5.cloned.1.call-update
  45.6 0.0 copy-start.2
  45.6 2.4 %fusion = bf16[1,1280,1024]{2,1,0:T(8,128)(2,1)} fusion(bf16[4,4,2,1280]{3,1,2,0:T(4,128)(2,1)S(1)} %all_gather.8, bf16[4,4,2,1024]{3,1,2,0:T(4,128)(2,1)S(1)} %fusion.33), kind=kOutput, calls=%fused_computation.2 | convolution fusion | flops 85196800 | bytes 2768896 | tf_op jit(solution)/shard_map/nesd,nesf->df/dot_general | solution.py:70
  48.0 0.0 copy-start.3
  48.0 30.6 %all-reduce.5.cloned.1.call-done = (bf16[4,4,2,1280]{3,1,2,0:T(4,128)(2,1)}, bf16[4,4,2,1280]{3,1,2,0:T(4,128)(2,1)}) async-done(((bf16[4,4,2,1280]{3,1,2,0:T(4,128)(2,1)}, bf16[4,4,2,1280]{3,1,2,0:T(4,128)(2,1)}), (bf16[4,4,2,1280]{3,1,2,0:T(4,128)(2,1)}, bf16[4,4,2,1280]{3,1,2,0:T(4,128)(2,1)})) %all-reduce.5.cloned.1.call-update) | async-done | bytes 163856
  78.6 1.4 constant_dynamic-slice_fusion.1
  80.0 0.6 copy.27
  80.6 4.6 %all-to-all-start.2 = ((bf16[1,4,2,1280]{3,2,0,1:T(2,128)(2,1)}), bf16[1,4,2,1280]{3,2,0,1:T(2,128)(2,1)S(1)}, u32[]{:S(2)}, u32[]{:S(2)}) async-start(bf16[1,4,2,1280]{3,2,0,1:T(2,128)(2,1)} %copy.27), calls=%async_computation.2 | async-start | bytes 40960 | tf_op jit(solution)/shard_map/all_to_all | solution.py:85
  85.2 1.4 constant_dynamic-slice_fusion
  86.6 0.6 copy.28
  87.2 3.6 %all-to-all-done.2 = bf16[1,4,2,1280]{3,2,0,1:T(2,128)(2,1)S(1)} async-done(((bf16[1,4,2,1280]{3,2,0,1:T(2,128)(2,1)}), bf16[1,4,2,1280]{3,2,0,1:T(2,128)(2,1)S(1)}, u32[]{:S(2)}, u32[]{:S(2)}) %all-to-all-start.2) | async-done | bytes 20512 | tf_op jit(solution)/shard_map/all_to_all | solution.py:85
  90.8 3.3 %all-to-all-start.3 = ((bf16[1,4,2,1280]{3,2,0,1:T(2,128)(2,1)}), bf16[1,4,2,1280]{3,2,0,1:T(2,128)(2,1)S(1)}, u32[]{:S(2)}, u32[]{:S(2)}) async-start(bf16[1,4,2,1280]{3,2,0,1:T(2,128)(2,1)} %copy.28), calls=%async_computation.3 | async-start | bytes 40960 | tf_op jit(solution)/shard_map/all_to_all | solution.py:45
  94.1 1.5 fusion.41
  95.6 0.0 copy-done.2
  95.6 0.2 fusion.22
  95.9 3.8 %all-to-all-done.3 = bf16[1,4,2,1280]{3,2,0,1:T(2,128)(2,1)S(1)} async-done(((bf16[1,4,2,1280]{3,2,0,1:T(2,128)(2,1)}), bf16[1,4,2,1280]{3,2,0,1:T(2,128)(2,1)S(1)}, u32[]{:S(2)}, u32[]{:S(2)}) %all-to-all-start.3) | async-done | bytes 20512 | tf_op jit(solution)/shard_map/all_to_all | solution.py:45
  99.7 1.5 multiply_reduce_fusion.1
  101.2 0.3 convolution_bitcast_fusion
  101.5 58.3 %psum.7 = f32[1280,8]{0,1:T(8,128)} all-reduce(f32[1280,8]{0,1:T(8,128)S(1)} %convolution_bitcast_fusion), channel_id=1, replica_groups=mesh['groups'=2,'expert'=4,'dp'=4] {'expert','dp'}, use_global_device_ids=true, to_apply=%region_8.0 | all-reduce | flops 10240 | bytes 81920 | tf_op jit(solution)/shard_map/psum | solution.py:98
  159.8 0.0 copy-done.3
  159.8 2.6 %fusion.11 = bf16[1,256,1280]{2,1,0:T(8,128)(2,1)} fusion(f32[256,1280]{1,0:T(8,128)} %fusion.41, bf16[1280,8]{0,1:T(8,128)(2,1)S(1)} %copy-done.3, f32[8,256]{1,0:T(8,128)S(1)} %fusion.22, f32[8,256]{1,0:T(8,128)S(1)} %get-tuple-element.13, f32[8]{0:T(128)S(1)} %get-tuple-element.5, f32[256]{0:T(256)S(1)} %get-tuple-element.4, ...), kind=kOutput, calls=%fused_computation.14 | convolution fusion | flops 5918720 | bytes 2014304 | tf_op jit(solution)/shard_map/ict,dc->itd/dot_general | solution.py:94
  (4 shorter events, 0.0 us)
Async XLA Ops:
  7.2 32.3 %copy-start = (bf16[1,1024,1280]{2,1,0:T(8,128)(2,1)S(1)}, bf16[1,1024,1280]{2,1,0:T(8,128)(2,1)}, u32[]{:S(2)}) copy-start(bf16[1,1024,1280]{2,1,0:T(8,128)(2,1)} %param.9) | copy-start | bytes 7864324
  11.0 11.9 %all-to-all-start.1 = ((bf16[1,4,2,1280]{3,2,0,1:T(2,128)(2,1)}), bf16[1,4,2,1280]{3,2,0,1:T(2,128)(2,1)S(1)}, u32[]{:S(2)}, u32[]{:S(2)}) async-start(bf16[1,4,2,1280]{3,2,0,1:T(2,128)(2,1)} %bitcast.6), calls=%async_computation.1 | async-start | bytes 40960 | tf_op jit(solution)/shard_map/all_to_all | solution.py:28
  23.0 8.9 %all-to-all-start = ((bf16[1,4,2,1280]{3,2,0,1:T(2,128)(2,1)}), bf16[1,4,2,1280]{3,2,0,1:T(2,128)(2,1)S(1)}, u32[]{:S(2)}, u32[]{:S(2)}) async-start(bf16[1,4,2,1280]{3,2,0,1:T(2,128)(2,1)} %bitcast.2), calls=%async_computation | async-start | bytes 40960 | tf_op jit(solution)/shard_map/all_to_all | solution.py:55
  26.2 52.4 %all-reduce.5.cloned.1.call-start = ((), (), s32[]{:S(2)}) async-start(), calls=%async_computation.4 | async-start | bytes 327680
  41.6 2.5 %copy-start.1 = (bf16[1,1280,1024]{2,1,0:T(8,128)(2,1)S(1)}, bf16[1,1280,1024]{2,1,0:T(8,128)(2,1)}, u32[]{:S(2)}) copy-start(bf16[1,1280,1024]{2,1,0:T(8,128)(2,1)} %param.8) | copy-start | bytes 7864324
  45.6 50.0 %copy-start.2 = (bf16[1,256,1280]{2,1,0:T(8,128)(2,1)S(1)}, bf16[1,256,1280]{2,1,0:T(8,128)(2,1)}, u32[]{:S(2)}) copy-start(bf16[1,256,1280]{2,1,0:T(8,128)(2,1)} %param.5) | copy-start | bytes 1966084
  48.0 111.7 %copy-start.3 = (bf16[1280,8]{0,1:T(8,128)(2,1)S(1)}, bf16[1280,8]{0,1:T(8,128)(2,1)}, u32[]{:S(2)}) copy-start(bf16[1280,8]{0,1:T(8,128)(2,1)} %param.7) | copy-start | bytes 61444
  80.6 10.2 %all-to-all-start.2 = ((bf16[1,4,2,1280]{3,2,0,1:T(2,128)(2,1)}), bf16[1,4,2,1280]{3,2,0,1:T(2,128)(2,1)S(1)}, u32[]{:S(2)}, u32[]{:S(2)}) async-start(bf16[1,4,2,1280]{3,2,0,1:T(2,128)(2,1)} %copy.27), calls=%async_computation.2 | async-start | bytes 40960 | tf_op jit(solution)/shard_map/all_to_all | solution.py:85
  90.8 8.9 %all-to-all-start.3 = ((bf16[1,4,2,1280]{3,2,0,1:T(2,128)(2,1)}), bf16[1,4,2,1280]{3,2,0,1:T(2,128)(2,1)S(1)}, u32[]{:S(2)}, u32[]{:S(2)}) async-start(bf16[1,4,2,1280]{3,2,0,1:T(2,128)(2,1)} %copy.28), calls=%async_computation.3 | async-start | bytes 40960 | tf_op jit(solution)/shard_map/all_to_all | solution.py:45
Sparse Core Ops, SparseCore 0:
  45.7 32.8 all-reduce.4
where the time goes:
time: 170 us; the launch traced here: 169 us
  blocking collectives  68.9 us (41%)
  waiting for transfers between devices  40.7 us (24%)
  matrix products  21.2 us (12%)
  starting transfers between devices  17.5 us (10%)
  between operations  14.1 us (8%)
  local copies, waits for them, and re-layouts  6.6 us (4%)
    psum x1, blocking collectives, local(): params_grad = lax.psum(local_params, ('expert', 'dp'))  58.3 us
    unnamed x2, waiting for transfers between devices  30.6 us
    all_to_all x1, starting transfers between devices, local(): lax.all_to_all(slot_in, 'expert', split_axis=1, concat_axis=1, tiled=True)  6.32 us
    all_gather x1, blocking collectives, local(): lax.all_gather(arrived, 'dp', axis=0, tiled=True)  5.29 us
    all_gather x1, blocking collectives, local(): shard_piece = lax.all_gather(sent_grads, 'dp', axis=0, tiled=True)  5.29 us
    all_to_all x1, starting transfers between devices, local(): lax.all_to_all(g_back, 'expert', split_axis=1, concat_axis=1, tiled=True)  4.6 us
    unnamed x11, local copies, waits for them, and re-layouts  4.03 us
    all_to_all x1, waiting for transfers between devices, local(): lax.all_to_all(summed, 'expert', split_axis=1, concat_axis=1, tiled=True)  3.81 us
  transfers between devices with their start and end apart: 5, of which 5 were waited for; matrix products, arithmetic and copies ran while one was open for 6% of the time, Pallas kernels for 0%

commit v1 on v0

v1 whole, which is shorter than its diff:
```python
import functools

import jax
import jax.numpy as jnp
from jax import lax
from jax.experimental import pallas as pl
from jax.experimental.pallas import tpu as pltpu
from jax.sharding import PartitionSpec as P

F32, BF16 = jnp.float32, jnp.bfloat16
MESH = pl.DeviceIdType.MESH
ROWS, PIECES = 4, 4
MSG = ROWS * PIECES
CHUNK = 16


def dot(a, b, contract, out=F32):
    return lax.dot_general(a, b, ((contract[:1], contract[1:]), ((), ())), preferred_element_type=out)


def pieces_of(width):
    step = -(-width // (PIECES * 128)) * 128
    return step, [(q * step, min(width, (q + 1) * step)) for q in range(PIECES)]


def select(messages, q):
    shape = (messages * ROWS, messages * MSG)
    row = lax.broadcasted_iota(jnp.int32, shape, 0)
    line = lax.broadcasted_iota(jnp.int32, shape, 1)
    half = (row >= messages * 2).astype(jnp.int32)
    inner = row - half * (messages * 2)
    target = (inner >> 1) * MSG + q * ROWS + half * 2 + (inner & 1)
    return (line == target).astype(BF16)


def pack(rows, messages):
    width = rows.shape[1]
    step, spans = pieces_of(width)
    total = None
    for q, (low, high) in enumerate(spans):
        piece = rows[:, low:high]
        if high - low < step:
            piece = jnp.concatenate([piece, jnp.zeros((rows.shape[0], step - high + low), BF16)], axis=1)
        part = dot(select(messages, q), piece, (0, 0))
        total = part if total is None else total + part
    return total.astype(BF16)


def kernel(
    experts, dp_size, tokens_ref, cot_ref, params_ref, inner_hbm, outer_hbm,
    gtok_ref, gparams_ref, x_ref, g_ref, hidden_ref, gpre_ref,
    inner_ref, outer_ref, send1, recv1, send2, recv2, part_a, part_b,
    load_sem, send_sem, recv_sem,
):
    peers = experts * dp_size
    expert = lax.axis_index("expert")
    dp = lax.axis_index("dp")
    me = expert * dp_size + dp
    width = tokens_ref.shape[1]
    step, spans = pieces_of(width)
    columns = params_ref.shape[0]
    half = width // 2

    load_inner = pltpu.make_async_copy(inner_hbm, inner_ref, load_sem.at[0])
    load_outer = pltpu.make_async_copy(outer_hbm, outer_ref, load_sem.at[1])
    load_inner.start()
    load_outer.start()

    def device(peer):
        return {"expert": lax.div(peer, dp_size), "dp": lax.rem(peer, dp_size)}

    barrier = pltpu.get_barrier_semaphore()

    @pl.loop(1, peers)
    def _(offset):
        pl.semaphore_signal(
            barrier, inc=1, device_id=device(lax.rem(me + offset, peers)), device_id_type=MESH
        )

    tokens = tokens_ref[...]
    logits = dot(params_ref[...], tokens, (1, 1))
    e_t = jnp.exp(logits - jnp.max(logits, axis=1, keepdims=True))
    dispatch_exact = e_t / jnp.sum(e_t, axis=1, keepdims=True)
    e_c = jnp.exp(logits - jnp.max(logits, axis=0, keepdims=True))
    combine_exact = e_c / jnp.sum(e_c, axis=0, keepdims=True)
    dispatch = dispatch_exact.astype(BF16)
    slot_in = dot(dispatch, tokens, (1, 0))
    g_slot_out = dot(combine_exact.astype(BF16), cot_ref[...], (1, 0))
    both = jnp.concatenate([slot_in, g_slot_out], axis=0).astype(BF16)
    send1[...] = pack(both, experts).reshape(experts, MSG, step)
    recv1[pl.ds(me, 1)] = send1[pl.ds(expert, 1)]

    pl.semaphore_wait(barrier, peers - 1)

    def exchange(index, source, target):
        @pl.loop(1, peers)
        def _(offset):
            peer = lax.rem(me + offset, peers)
            pltpu.make_async_remote_copy(
                src_ref=source(peer), dst_ref=target.at[me], send_sem=send_sem.at[index],
                recv_sem=recv_sem.at[index], device_id=device(peer), device_id_type=MESH,
            ).start()

    def wait(index, target, count):
        whole = target.at[pl.ds(0, count)]
        copy = pltpu.make_async_remote_copy(
            src_ref=whole, dst_ref=whole, send_sem=send_sem.at[index],
            recv_sem=recv_sem.at[index], device_id={"expert": expert, "dp": dp}, device_id_type=MESH,
        )
        copy.wait_recv()
        copy.wait_send()

    exchange(0, lambda peer: send1.at[lax.div(peer, dp_size)], recv1)
    wait(0, recv1, peers - 1)

    chunk = min(CHUNK, peers)
    lines = chunk * 2

    @pl.loop(0, peers // chunk)
    def _(index):
        block = recv1[pl.ds(index * chunk, chunk)].reshape(chunk * MSG, step)
        at = pl.ds(pl.multiple_of(index * lines, lines), lines)
        for q, (low, high) in enumerate(spans):
            piece = dot(select(chunk, q), block[:, : high - low], (1, 0)).astype(BF16)
            x_ref[at, low:high] = piece[:lines]
            g_ref[at, low:high] = piece[lines:]

    load_inner.wait()
    load_outer.wait()
    rows, g_rows = x_ref[...], g_ref[...]
    pre = dot(rows, inner_ref[...], (1, 0))
    g_hidden = dot(g_rows, outer_ref[...], (1, 1))
    scale = 0.7978845608028654
    tanh = jnp.tanh(scale * (pre + 0.044715 * (pre * pre * pre)))
    gate = 0.5 * (1.0 + tanh)
    hidden = (pre * gate).astype(BF16)
    slope = gate + (0.5 * pre) * (1.0 - tanh * tanh) * (scale * (1.0 + 0.134145 * (pre * pre)))
    g_pre = (g_hidden * slope).astype(BF16)
    hidden_ref[...] = hidden
    gpre_ref[...] = g_pre
    out_part = dot(hidden, outer_ref[...], (1, 0)).astype(BF16)
    g_part = dot(g_pre, inner_ref[...], (1, 1)).astype(BF16)
    for index in range(peers // chunk):
        at = slice(index * lines, (index + 1) * lines)
        both = jnp.concatenate([out_part[at], g_part[at]], axis=0)
        send2[index * chunk : (index + 1) * chunk] = pack(both, chunk).reshape(chunk, MSG, step)
    recv2[pl.ds(me, 1)] = send2[pl.ds(me, 1)]
    exchange(1, lambda peer: send2.at[peer], recv2)
    wait(1, recv2, peers - 1)

    block = recv2[...].reshape(peers * MSG, step)
    shape = (2 * columns, peers * MSG)
    row = lax.broadcasted_iota(jnp.int32, shape, 0)
    line = lax.broadcasted_iota(jnp.int32, shape, 1)
    second = (row >= columns).astype(jnp.int32)
    column = row - second * columns
    per_expert = dp_size * MSG
    wanted = second * 2 + (column & 1)
    base = (column >> 1) * per_expert
    inside = (line >= base) & (line < base + per_expert)
    sums = []
    for q, (low, high) in enumerate(spans):
        take = (inside & ((line & (MSG - 1)) == wanted + q * ROWS)).astype(BF16)
        sums.append(dot(take, block[:, : high - low], (1, 0)))
    total = jnp.concatenate(sums, axis=1)
    slot_out = total[:columns].astype(BF16)
    g_slot_in = total[columns:].astype(BF16)

    g_combine = dot(slot_out, cot_ref[...], (1, 1))
    g_logit = combine_exact * (
        g_combine - jnp.sum(combine_exact * g_combine, axis=0, keepdims=True)
    )
    g_dispatch = dot(g_slot_in, tokens, (1, 1))
    g_logit = g_logit + dispatch_exact * (
        g_dispatch - jnp.sum(dispatch_exact * g_dispatch, axis=1, keepdims=True)
    )
    g_logits = g_logit.astype(BF16)
    local = dot(g_logits, tokens, (1, 0))

    def fold(values):
        return jnp.concatenate([values[:, :half], values[:, half:]], axis=0).astype(BF16)

    def spread(index, target, own, axis, size):
        @pl.loop(1, size)
        def _(offset):
            other = lax.rem(own + offset, size)
            where = {"expert": expert, "dp": dp}
            where[axis] = other
            pltpu.make_async_remote_copy(
                src_ref=target.at[own], dst_ref=target.at[own], send_sem=send_sem.at[index],
                recv_sem=recv_sem.at[index], device_id=where, device_id_type=MESH,
            ).start()

    def add(target, size):
        folded = target[0].astype(F32)
        for index in range(1, size):
            folded = folded + target[index].astype(F32)
        return folded

    part_a[pl.ds(dp, 1)] = fold(local)[None]
    spread(2, part_a, dp, "dp", dp_size)
    left = jnp.concatenate([dispatch_exact, g_logits.astype(F32)], axis=0).astype(BF16)
    right = jnp.concatenate([g_slot_in.astype(F32), params_ref[...].astype(F32)], axis=0).astype(BF16)
    gtok_ref[...] = dot(left, right, (0, 0)).astype(BF16)
    wait(2, part_a, dp_size - 1)
    part_b[pl.ds(expert, 1)] = add(part_a, dp_size).astype(BF16)[None]
    spread(3, part_b, expert, "expert", experts)
    wait(3, part_b, experts - 1)
    folded = add(part_b, experts)
    gparams_ref[:, :half] = folded[:columns]
    gparams_ref[:, half:] = folded[columns:]


def local(tokens, cotangent, slot_params, inner_weight, outer_weight):
    width = tokens.shape[2]
    patches = tokens.shape[1]
    columns = slot_params.shape[1]
    experts = lax.axis_size("expert")
    dp_size = lax.axis_size("dp")
    peers = experts * dp_size
    units = inner_weight.shape[2]
    rows = peers * 2
    step, _ = pieces_of(width)
    vmem = pl.BlockSpec(memory_space=pltpu.VMEM)
    hbm = pl.BlockSpec(memory_space=pl.ANY)
    shape = jax.ShapeDtypeStruct
    g_tokens, g_params, x, g, hidden, g_pre = pl.pallas_call(
        functools.partial(kernel, experts, dp_size),
        out_shape=[
            shape((patches, width), BF16),
            shape((columns, width), F32),
            shape((rows, width), BF16),
            shape((rows, width), BF16),
            shape((rows, units), BF16),
            shape((rows, units), BF16),
        ],
        in_specs=[vmem, vmem, vmem, hbm, hbm],
        out_specs=[vmem] * 6,
        scratch_shapes=[
            pltpu.VMEM((width, units), BF16),
            pltpu.VMEM((units, width), BF16),
            pltpu.VMEM((experts, MSG, step), BF16),
            pltpu.VMEM((peers, MSG, step), BF16),
            pltpu.VMEM((peers, MSG, step), BF16),
            pltpu.VMEM((peers, MSG, step), BF16),
            pltpu.VMEM((dp_size, 2 * columns, width // 2), BF16),
            pltpu.VMEM((experts, 2 * columns, width // 2), BF16),
            pltpu.SemaphoreType.DMA((2,)),
            pltpu.SemaphoreType.DMA((4,)),
            pltpu.SemaphoreType.DMA((4,)),
        ],
        compiler_params=pltpu.CompilerParams(
            collective_id=0, has_side_effects=True, vmem_limit_bytes=48 * 1024 * 1024
        ),
    )(tokens[0], cotangent[0], slot_params.T, inner_weight[0], outer_weight[0])
    grad_inner = dot(x, g_pre, (0, 0)).astype(BF16)
    grad_outer = dot(hidden, g, (0, 0)).astype(BF16)
    return g_tokens[None], g_params.T, grad_inner[None], grad_outer[None]


def solution(mesh):
    return jax.shard_map(
        local,
        mesh=mesh,
        in_specs=(
            P(("groups", "expert", "dp"), None, None),
            P(("groups", "expert", "dp"), None, None),
            P(),
            P("expert", None, "dp"),
            P("expert", "dp", None),
        ),
        out_specs=(
            P(("groups", "expert", "dp"), None, None),
            P("groups", None),
            P(("groups", "expert"), None, "dp"),
            P(("groups", "expert"), "dp", None),
        ),
        check_vma=False,
    )
```

time: 170 us -> 40.9 us (0.24)
  blocking collectives: 68.9 us -> 0 us
  waiting for transfers between devices: 40.7 us -> 0 us
  Pallas kernels: 0 us -> 29.1 us
  starting transfers between devices: 17.5 us -> 0 us
  matrix products: 21.2 us -> 4.72 us
  between operations: 14.1 us -> 0.65 us
    psum x1 -> x0, blocking collectives: 58.3 us -> none  [local(): params_grad = lax.psum(local_params, ('expert', 'dp'))]
    unnamed x2 -> x0, waiting for transfers between devices: 30.6 us -> none
    pallas_call x0 -> x1, Pallas kernels: none -> 29.1 us  [local(): pl.pallas_call(functools.partial(kernel, experts, dp_size), out_shape=[sh...]
    all_to_all x4 -> x0, starting transfers between devices: 17.4 us -> none  [the longest x1 6.32 us: local(): lax.all_to_all(slot_in, 'expert', split_axis=1, concat_axis=1, tiled=True)]
    dot_general x14 -> x2, matrix products: 21.2 us -> 4.72 us  [dot(): lax.dot_general(a, b, ((contract[:1], contract[1:]), ((), ())), preferred...]
    all_gather x2 -> x0, blocking collectives: 10.6 us -> none  [the longest x1 5.29 us: local(): lax.all_gather(arrived, 'dp', axis=0, tiled=True)]
    all_to_all x4 -> x0, waiting for transfers between devices: 10.1 us -> none  [the longest x1 3.81 us: local(): lax.all_to_all(summed, 'expert', split_axis=1, concat_axis=1, tiled=True)]
    unnamed x11 -> x10, local copies, waits for them, and re-layouts: 4.03 us -> 6.09 us
  transfers between devices with their start and end apart: 5 -> 0, of which waited for: 5 -> 0; matrix products, arithmetic and copies ran while one was open for 6% -> 0% of each run, Pallas kernels for 0% -> 0%
where the time goes in v1:
time: 40.9 us; the launch traced here: 40.6 us
  Pallas kernels  29.1 us (71%)
  local copies, waits for them, and re-layouts  6.09 us (15%)
  matrix products  4.72 us (12%)
  between operations  0.65 us (2%)
    pallas_call x1, Pallas kernels, local(): pl.pallas_call(functools.partial(kernel, experts, dp_size), out_shape=[sh...  29.1 us
    unnamed x10, local copies, waits for them, and re-layouts  6.09 us
    dot_general x2, matrix products, dot(): lax.dot_general(a, b, ((contract[:1], contract[1:]), ((), ())), preferred...  4.72 us

profile of v1, /device:TPU:0, one launch (start us, length us, event | category | flops | bytes accessed | tf_op | source)
XLA Modules:
  0.0 40.6 jit_solution(4536386828778737702)
XLA Ops:
  0.6 0.0 copy-start
  0.6 1.7 %copy-done = bf16[1,1280,1024]{2,1,0:T(8,128)(2,1)S(1)} copy-done((bf16[1,1280,1024]{2,1,0:T(8,128)(2,1)S(1)}, bf16[1,1280,1024]{2,1,0:T(8,128)(2,1)}, u32[]{:S(2)}) %copy-start) | copy-done | bytes 2621464
  2.4 0.0 copy-start.1
  2.4 1.1 %copy-done.1 = bf16[1,256,1280]{2,1,0:T(8,128)(2,1)S(1)} copy-done((bf16[1,256,1280]{2,1,0:T(8,128)(2,1)S(1)}, bf16[1,256,1280]{2,1,0:T(8,128)(2,1)}, u32[]{:S(2)}) %copy-start.1) | copy-done | bytes 655384
  3.5 0.0 copy-start.2
  3.5 1.1 %copy-done.2 = bf16[1,256,1280]{2,1,0:T(8,128)(2,1)S(1)} copy-done((bf16[1,256,1280]{2,1,0:T(8,128)(2,1)S(1)}, bf16[1,256,1280]{2,1,0:T(8,128)(2,1)}, u32[]{:S(2)}) %copy-start.2) | copy-done | bytes 655384
  4.5 0.0 copy-start.3
  4.6 0.7 %copy-done.3 = bf16[1280,8]{0,1:T(8,128)(2,1)S(1)} copy-done((bf16[1280,8]{0,1:T(8,128)(2,1)S(1)}, bf16[1280,8]{0,1:T(8,128)(2,1)}, u32[]{:S(2)}) %copy-start.3) | copy-done | bytes 20504
  5.3 29.1 %shard_map.84 = (bf16[256,1280]{1,0:T(8,128)(2,1)S(1)}, f32[8,1280]{1,0:T(8,128)S(1)}, bf16[32,1280]{1,0:T(8,128)(2,1)S(1)}, bf16[32,1280]{1,0:T(8,128)(2,1)S(1)...) custom-call(bf16[256,1280]{1,0:T(8,128)(2,1)S(1)} %bitcast.17, bf16[256,1280]{1,0:T(8,128)(2,1)S(1)} %bitcast.18, ...), custom_call_target="tpu_custom_call" | custom-call | tf_op jit(solution)/shard_map/pallas_call | solution.py:227
  34.4 2.4 %fusion = bf16[1,1280,1024]{2,1,0:T(8,128)(2,1)} fusion(bf16[32,1280]{1,0:T(8,128)(2,1)S(1)} %get-tuple-element.12, bf16[32,1024]{1,0:T(8,128)(2,1)S(1)} %get-tuple-element.13), kind=kOutput, calls=%fused_computation.2 | convolution fusion | flops 85196800 | bytes 2768896 | tf_op jit(solution)/shard_map/dot_general | solution.py:18
  36.8 2.4 %fusion.1 = bf16[1,1024,1280]{2,1,0:T(8,128)(2,1)} fusion(bf16[32,1024]{1,0:T(8,128)(2,1)S(1)} %get-tuple-element.14, bf16[32,1280]{1,0:T(8,128)(2,1)S(1)} %get-tuple-element.15), kind=kOutput, calls=%fused_computation.3 | convolution fusion | flops 85196800 | bytes 2768896 | tf_op jit(solution)/shard_map/dot_general | solution.py:18
  39.1 0.8 %copy.11 = bf16[1,256,1280]{2,1,0:T(8,128)(2,1)} copy(bf16[1,256,1280]{2,1,0:T(8,128)(2,1)S(1)} %bitcast.16) | data formatting | bytes 1310720
  40.0 0.6 %copy.12 = f32[1280,8]{0,1:T(8,128)} copy(f32[1280,8]{0,1:T(8,128)S(1)} %bitcast.19) | data formatting | bytes 81920
Async XLA Ops:
  0.6 1.7 %copy-start = (bf16[1,1280,1024]{2,1,0:T(8,128)(2,1)S(1)}, bf16[1,1280,1024]{2,1,0:T(8,128)(2,1)}, u32[]{:S(2)}) copy-start(bf16[1,1280,1024]{2,1,0:T(8,128)(2,1)} %param.8) | copy-start | bytes 7864324
  2.4 1.1 %copy-start.1 = (bf16[1,256,1280]{2,1,0:T(8,128)(2,1)S(1)}, bf16[1,256,1280]{2,1,0:T(8,128)(2,1)}, u32[]{:S(2)}) copy-start(bf16[1,256,1280]{2,1,0:T(8,128)(2,1)} %param.5) | copy-start | bytes 1966084
  3.5 1.1 %copy-start.2 = (bf16[1,256,1280]{2,1,0:T(8,128)(2,1)S(1)}, bf16[1,256,1280]{2,1,0:T(8,128)(2,1)}, u32[]{:S(2)}) copy-start(bf16[1,256,1280]{2,1,0:T(8,128)(2,1)} %param.6) | copy-start | bytes 1966084
  4.5 0.7 %copy-start.3 = (bf16[1280,8]{0,1:T(8,128)(2,1)S(1)}, bf16[1280,8]{0,1:T(8,128)(2,1)}, u32[]{:S(2)}) copy-start(bf16[1280,8]{0,1:T(8,128)(2,1)} %param.7) | copy-start | bytes 61444

commit v2 on v1

--- a/solution.py
+++ b/solution.py
@@ -12,6 +12,7 @@
 ROWS, PIECES = 4, 4
 MSG = ROWS * PIECES
 CHUNK = 16
+VMEM_BYTES = 60 * 1024 * 1024
 
 
 def dot(a, b, contract, out=F32):
@@ -47,10 +48,11 @@
 
 
 def kernel(
-    experts, dp_size, tokens_ref, cot_ref, params_ref, inner_hbm, outer_hbm,
-    gtok_ref, gparams_ref, x_ref, g_ref, hidden_ref, gpre_ref,
-    inner_ref, outer_ref, send1, recv1, send2, recv2, part_a, part_b,
-    load_sem, send_sem, recv_sem,
+    experts, dp_size, tokens_hbm, cot_hbm, params_hbm, inner_hbm, outer_hbm,
+    x_hbm, g_hbm, hidden_hbm, gpre_hbm, left_hbm, right_hbm, gparams_hbm,
+    x_ref, g_ref, hidden_ref, gpre_ref, left_ref, right_ref, gparams_ref,
+    tokens_ref, cot_ref, params_ref, inner_ref, outer_ref, send1, recv1, send2, recv2, part_a, part_b,
+    load_sem, store_sem, send_sem, recv_sem,
 ):
     peers = experts * dp_size
     expert = lax.axis_index("expert")
@@ -61,10 +63,18 @@
     columns = params_ref.shape[0]
     half = width // 2
 
-    load_inner = pltpu.make_async_copy(inner_hbm, inner_ref, load_sem.at[0])
-    load_outer = pltpu.make_async_copy(outer_hbm, outer_ref, load_sem.at[1])
-    load_inner.start()
-    load_outer.start()
+    pairs = (
+        (params_hbm, params_ref), (tokens_hbm, tokens_ref), (cot_hbm, cot_ref),
+        (inner_hbm, inner_ref), (outer_hbm, outer_ref),
+    )
+    loads = [pltpu.make_async_copy(a, b, load_sem.at[i]) for i, (a, b) in enumerate(pairs)]
+    pairs = (
+        (x_ref, x_hbm), (g_ref, g_hbm), (hidden_ref, hidden_hbm), (gpre_ref, gpre_hbm),
+        (left_ref, left_hbm), (right_ref, right_hbm), (gparams_ref, gparams_hbm),
+    )
+    stores = [pltpu.make_async_copy(a, b, store_sem.at[i]) for i, (a, b) in enumerate(pairs)]
+    for load in loads:
+        load.start()
 
     def device(peer):
         return {"expert": lax.div(peer, dp_size), "dp": lax.rem(peer, dp_size)}
@@ -77,6 +87,8 @@
             barrier, inc=1, device_id=device(lax.rem(me + offset, peers)), device_id_type=MESH
         )
 
+    loads[0].wait()
+    loads[1].wait()
     tokens = tokens_ref[...]
     logits = dot(params_ref[...], tokens, (1, 1))
     e_t = jnp.exp(logits - jnp.max(logits, axis=1, keepdims=True))
@@ -85,6 +97,7 @@
     combine_exact = e_c / jnp.sum(e_c, axis=0, keepdims=True)
     dispatch = dispatch_exact.astype(BF16)
     slot_in = dot(dispatch, tokens, (1, 0))
+    loads[2].wait()
     g_slot_out = dot(combine_exact.astype(BF16), cot_ref[...], (1, 0))
     both = jnp.concatenate([slot_in, g_slot_out], axis=0).astype(BF16)
     send1[...] = pack(both, experts).reshape(experts, MSG, step)
@@ -125,8 +138,10 @@
             x_ref[at, low:high] = piece[:lines]
             g_ref[at, low:high] = piece[lines:]
 
-    load_inner.wait()
-    load_outer.wait()
+    loads[3].wait()
+    loads[4].wait()
+    stores[0].start()
+    stores[1].start()
     rows, g_rows = x_ref[...], g_ref[...]
     pre = dot(rows, inner_ref[...], (1, 0))
     g_hidden = dot(g_rows, outer_ref[...], (1, 1))
@@ -138,6 +153,8 @@
     g_pre = (g_hidden * slope).astype(BF16)
     hidden_ref[...] = hidden
     gpre_ref[...] = g_pre
+    stores[2].start()
+    stores[3].start()
     out_part = dot(hidden, outer_ref[...], (1, 0)).astype(BF16)
     g_part = dot(g_pre, inner_ref[...], (1, 1)).astype(BF16)
     for index in range(peers // chunk):
@@ -199,9 +216,11 @@
 
     part_a[pl.ds(dp, 1)] = fold(local)[None]
     spread(2, part_a, dp, "dp", dp_size)
-    left = jnp.concatenate([dispatch_exact, g_logits.astype(F32)], axis=0).astype(BF16)
-    right = jnp.concatenate([g_slot_in.astype(F32), params_ref[...].astype(F32)], axis=0).astype(BF16)
-    gtok_ref[...] = dot(left, right, (0, 0)).astype(BF16)
+    left_ref[...] = jnp.concatenate([dispatch_exact, g_logits.astype(F32)], axis=0).astype(BF16)
+    right_ref[:columns] = g_slot_in
+    right_ref[columns:] = params_ref[...]
+    stores[4].start()
+    stores[5].start()
     wait(2, part_a, dp_size - 1)
     part_b[pl.ds(expert, 1)] = add(part_a, dp_size).astype(BF16)[None]
     spread(3, part_b, expert, "expert", experts)
@@ -209,6 +228,49 @@
     folded = add(part_b, experts)
     gparams_ref[:, :half] = folded[:columns]
     gparams_ref[:, half:] = folded[columns:]
+    stores[6].start()
+    for store in stores:
+        store.wait()
+
+
+def weight_kernel(
+    x_hbm, g_hbm, hidden_hbm, gpre_hbm, left_hbm, right_hbm, gparams_hbm,
+    gtok_hbm, gout_hbm, ginner_hbm, gouter_hbm,
+    x_ref, g_ref, hidden_ref, gpre_ref, left_ref, right_ref, gparams_ref,
+    gtok_ref, ginner_ref, gouter_ref, load_sem, store_sem,
+):
+    pairs = (
+        (x_hbm, x_ref), (gpre_hbm, gpre_ref), (hidden_hbm, hidden_ref), (g_hbm, g_ref),
+        (left_hbm, left_ref), (right_hbm, right_ref), (gparams_hbm, gparams_ref),
+    )
+    loads = [pltpu.make_async_copy(a, b, load_sem.at[i]) for i, (a, b) in enumerate(pairs)]
+    for load in loads:
+        load.start()
+    stores = []
+
+    def product(left, right, out_ref, out_hbm):
+        for low in range(0, out_ref.shape[0], 256):
+            at = slice(low, min(low + 256, out_ref.shape[0]))
+            out_ref[at] = dot(left[:, at], right[...], (0, 0)).astype(BF16)
+            stores.append(pltpu.make_async_copy(
+                out_ref.at[at], out_hbm.at[at], store_sem.at[len(stores)]
+            ))
+            stores[-1].start()
+
+    loads[0].wait()
+    loads[1].wait()
+    product(x_ref, gpre_ref, ginner_ref, ginner_hbm)
+    loads[2].wait()
+    loads[3].wait()
+    product(hidden_ref, g_ref, gouter_ref, gouter_hbm)
+    loads[4].wait()
+    loads[5].wait()
+    product(left_ref, right_ref, gtok_ref, gtok_hbm)
+    loads[6].wait()
+    stores.append(pltpu.make_async_copy(gparams_ref, gout_hbm, store_sem.at[len(stores)]))
+    stores[-1].start()
+    for store in stores:
+        store.wait()
 
 
 def local(tokens, cotangent, slot_params, inner_weight, outer_weight):
@@ -221,22 +283,27 @@
     units = inner_weight.shape[2]
     rows = peers * 2
     step, _ = pieces_of(width)
-    vmem = pl.BlockSpec(memory_space=pltpu.VMEM)
     hbm = pl.BlockSpec(memory_space=pl.ANY)
     shape = jax.ShapeDtypeStruct
-    g_tokens, g_params, x, g, hidden, g_pre = pl.pallas_call(
+    small = (
+        shape((rows, width), BF16),
+        shape((rows, width), BF16),
+        shape((rows, units), BF16),
+        shape((rows, units), BF16),
+        shape((2 * columns, patches), BF16),
+        shape((2 * columns, width), BF16),
+        shape((columns, width), F32),
+    )
+    held = [pltpu.VMEM(s.shape, s.dtype) for s in small]
+    small = pl.pallas_call(
         functools.partial(kernel, experts, dp_size),
-        out_shape=[
-            shape((patches, width), BF16),
-            shape((columns, width), F32),
-            shape((rows, width), BF16),
-            shape((rows, width), BF16),
-            shape((rows, units), BF16),
-            shape((rows, units), BF16),
-        ],
-        in_specs=[vmem, vmem, vmem, hbm, hbm],
-        out_specs=[vmem] * 6,
-        scratch_shapes=[
+        out_shape=small,
+        in_specs=[hbm] * 5,
+        out_specs=[hbm] * 7,
+        scratch_shapes=held + [
+            pltpu.VMEM((patches, width), BF16),
+            pltpu.VMEM((patches, width), BF16),
+            pltpu.VMEM((columns, width), BF16),
             pltpu.VMEM((width, units), BF16),
             pltpu.VMEM((units, width), BF16),
             pltpu.VMEM((experts, MSG, step), BF16),
@@ -245,16 +312,36 @@
             pltpu.VMEM((peers, MSG, step), BF16),
             pltpu.VMEM((dp_size, 2 * columns, width // 2), BF16),
             pltpu.VMEM((experts, 2 * columns, width // 2), BF16),
-            pltpu.SemaphoreType.DMA((2,)),
+            pltpu.SemaphoreType.DMA((5,)),
+            pltpu.SemaphoreType.DMA((7,)),
             pltpu.SemaphoreType.DMA((4,)),
             pltpu.SemaphoreType.DMA((4,)),
         ],
         compiler_params=pltpu.CompilerParams(
-            collective_id=0, has_side_effects=True, vmem_limit_bytes=48 * 1024 * 1024
+            collective_id=0, has_side_effects=True, vmem_limit_bytes=VMEM_BYTES
         ),
     )(tokens[0], cotangent[0], slot_params.T, inner_weight[0], outer_weight[0])
-    grad_inner = dot(x, g_pre, (0, 0)).astype(BF16)
-    grad_outer = dot(hidden, g, (0, 0)).astype(BF16)
+    results = (
+        shape((patches, width), BF16),
+        shape((columns, width), F32),
+        shape((width, units), BF16),
+        shape((units, width), BF16),
+    )
+    store_count = 1 + sum(-(-n // 256) for n in (patches, width, units))
+    g_tokens, g_params, grad_inner, grad_outer = pl.pallas_call(
+        weight_kernel,
+        out_shape=results,
+        in_specs=[hbm] * 7,
+        out_specs=[hbm] * 4,
+        scratch_shapes=held + [
+            pltpu.VMEM((patches, width), BF16),
+            pltpu.VMEM((width, units), BF16),
+            pltpu.VMEM((units, width), BF16),
+            pltpu.SemaphoreType.DMA((7,)),
+            pltpu.SemaphoreType.DMA((store_count,)),
+        ],
+        compiler_params=pltpu.CompilerParams(vmem_limit_bytes=VMEM_BYTES),
+    )(*small)
     return g_tokens[None], g_params.T, grad_inner[None], grad_outer[None]
 
 

time: 40.9 us -> 34.7 us (0.85)
  local copies, waits for them, and re-layouts: 6.09 us -> 0 us
  Pallas kernels: 29.1 us -> 33.9 us
  matrix products: 4.72 us -> 0 us
    unnamed x10 -> x0, local copies, waits for them, and re-layouts: 6.09 us -> none
    pallas_call x1 -> x2, Pallas kernels: 29.1 us -> 33.9 us  [the longest x1 29.8 us: local(): pl.pallas_call(functools.partial(kernel, experts, dp_size), out_shape=sma...]
    dot_general x2 -> x0, matrix products: 4.72 us -> none  [dot(): lax.dot_general(a, b, ((contract[:1], contract[1:]), ((), ())), preferred...]
where the time goes in v2:
time: 34.7 us; the launch traced here: 34.5 us
  Pallas kernels  33.9 us (98%)
  between operations  0.64 us (2%)
    pallas_call x1, Pallas kernels, local(): pl.pallas_call(functools.partial(kernel, experts, dp_size), out_shape=sma...  29.8 us
    pallas_call x1, Pallas kernels, local(): pl.pallas_call(weight_kernel, out_shape=results, in_specs=[hbm] * 7, out_...  4.08 us

profile of v2, /device:TPU:0, one launch (start us, length us, event | category | flops | bytes accessed | tf_op | source)
XLA Modules:
  0.0 34.5 jit_solution(1263137506421250172)
XLA Ops:
  0.6 29.8 %shard_map.84 = (bf16[32,1280]{1,0:T(8,128)(2,1)}, bf16[32,1280]{1,0:T(8,128)(2,1)}, bf16[32,1024]{1,0:T(8,128)(2,1)}, bf16[32,1024]{1,0:T(8,128)(2,1)}, bf16[16...) custom-call(bf16[256,1280]{1,0:T(8,128)(2,1)} %bitcast.11, bf16[256,1280]{1,0:T(8,128)(2,1)} %bitcast.12, ...), custom_call_target="tpu_custom_call" | custom-call | tf_op jit(solution)/shard_map/pallas_call | solution.py:298
  30.4 4.1 %shard_map.85 = (bf16[256,1280]{1,0:T(8,128)(2,1)}, f32[8,1280]{1,0:T(8,128)}, bf16[1280,1024]{1,0:T(8,128)(2,1)}, bf16[1024,1280]{1,0:T(8,128)(2,1)}) custom-call(bf16[32,1280]{1,0:T(8,128)(2,1)} %get-tuple-element.15.x_hbm, bf16[32,1280]{1,0:T(8,128)(2,1)} %get-tuple-element.16.g_hbm, bf16[32,1024]{1,0:T(8,128)(2,1)} %get-tuple-element.17.hidden_hbm, ...), custom_call_target="tpu_custom_call" | custom-call | tf_op jit(solution)/shard_map/pallas_call | solution.py:331

commit v3 on v2

--- a/solution.py
+++ b/solution.py
@@ -12,7 +12,7 @@
 ROWS, PIECES = 4, 4
 MSG = ROWS * PIECES
 CHUNK = 16
-VMEM_BYTES = 60 * 1024 * 1024
+VMEM_BYTES = 54500 * 1024
 
 
 def dot(a, b, contract, out=F32):
@@ -24,17 +24,17 @@
     return step, [(q * step, min(width, (q + 1) * step)) for q in range(PIECES)]
 
 
-def select(messages, q):
+def select(messages):
     shape = (messages * ROWS, messages * MSG)
     row = lax.broadcasted_iota(jnp.int32, shape, 0)
     line = lax.broadcasted_iota(jnp.int32, shape, 1)
     half = (row >= messages * 2).astype(jnp.int32)
     inner = row - half * (messages * 2)
-    target = (inner >> 1) * MSG + q * ROWS + half * 2 + (inner & 1)
-    return (line == target).astype(BF16)
-
-
-def pack(rows, messages):
+    shift = line - ((inner >> 1) * MSG + half * 2 + (inner & 1))
+    return [(shift == q * ROWS).astype(BF16) for q in range(PIECES)]
+
+
+def pack(rows, messages, chosen):
     width = rows.shape[1]
     step, spans = pieces_of(width)
     total = None
@@ -42,17 +42,16 @@
         piece = rows[:, low:high]
         if high - low < step:
             piece = jnp.concatenate([piece, jnp.zeros((rows.shape[0], step - high + low), BF16)], axis=1)
-        part = dot(select(messages, q), piece, (0, 0))
+        part = dot(chosen[q], piece, (0, 0))
         total = part if total is None else total + part
     return total.astype(BF16)
 
 
 def kernel(
     experts, dp_size, tokens_hbm, cot_hbm, params_hbm, inner_hbm, outer_hbm,
-    x_hbm, g_hbm, hidden_hbm, gpre_hbm, left_hbm, right_hbm, gparams_hbm,
     x_ref, g_ref, hidden_ref, gpre_ref, left_ref, right_ref, gparams_ref,
     tokens_ref, cot_ref, params_ref, inner_ref, outer_ref, send1, recv1, send2, recv2, part_a, part_b,
-    load_sem, store_sem, send_sem, recv_sem,
+    load_sem, send_sem, recv_sem,
 ):
     peers = experts * dp_size
     expert = lax.axis_index("expert")
@@ -68,24 +67,38 @@
         (inner_hbm, inner_ref), (outer_hbm, outer_ref),
     )
     loads = [pltpu.make_async_copy(a, b, load_sem.at[i]) for i, (a, b) in enumerate(pairs)]
-    pairs = (
-        (x_ref, x_hbm), (g_ref, g_hbm), (hidden_ref, hidden_hbm), (gpre_ref, gpre_hbm),
-        (left_ref, left_hbm), (right_ref, right_hbm), (gparams_ref, gparams_hbm),
-    )
-    stores = [pltpu.make_async_copy(a, b, store_sem.at[i]) for i, (a, b) in enumerate(pairs)]
     for load in loads:
         load.start()
 
-    def device(peer):
-        return {"expert": lax.div(peer, dp_size), "dp": lax.rem(peer, dp_size)}
+    def shifted(own, offset, size):
+        moved = own + offset
+        return jnp.where(moved >= size, moved - size, moved)
+
+    def every_peer(body):
+        if peers <= CHUNK:
+            for across in range(experts):
+                for along in range(dp_size):
+                    if across or along:
+                        body(shifted(expert, across, experts), shifted(dp, along, dp_size))
+        else:
+            @pl.loop(1, peers)
+            def _(offset):
+                body(
+                    shifted(expert, lax.div(offset, dp_size), experts),
+                    shifted(dp, lax.rem(offset, dp_size), dp_size),
+                )
 
     barrier = pltpu.get_barrier_semaphore()
 
-    @pl.loop(1, peers)
-    def _(offset):
+    def greet(to_expert, to_dp):
         pl.semaphore_signal(
-            barrier, inc=1, device_id=device(lax.rem(me + offset, peers)), device_id_type=MESH
+            barrier, inc=1, device_id={"expert": to_expert, "dp": to_dp}, device_id_type=MESH
         )
+
+    every_peer(greet)
+    chunk = min(CHUNK, peers)
+    lines = chunk * 2
+    of_experts, of_chunk = select(experts), select(chunk)
 
     loads[0].wait()
     loads[1].wait()
@@ -100,19 +113,20 @@
     loads[2].wait()
     g_slot_out = dot(combine_exact.astype(BF16), cot_ref[...], (1, 0))
     both = jnp.concatenate([slot_in, g_slot_out], axis=0).astype(BF16)
-    send1[...] = pack(both, experts).reshape(experts, MSG, step)
+    send1[...] = pack(both, experts, of_experts).reshape(experts, MSG, step)
     recv1[pl.ds(me, 1)] = send1[pl.ds(expert, 1)]
 
     pl.semaphore_wait(barrier, peers - 1)
 
     def exchange(index, source, target):
-        @pl.loop(1, peers)
-        def _(offset):
-            peer = lax.rem(me + offset, peers)
+        def send(to_expert, to_dp):
             pltpu.make_async_remote_copy(
-                src_ref=source(peer), dst_ref=target.at[me], send_sem=send_sem.at[index],
-                recv_sem=recv_sem.at[index], device_id=device(peer), device_id_type=MESH,
+                src_ref=source(to_expert, to_dp), dst_ref=target.at[me],
+                send_sem=send_sem.at[index], recv_sem=recv_sem.at[index],
+                device_id={"expert": to_expert, "dp": to_dp}, device_id_type=MESH,
             ).start()
+
+        every_peer(send)
 
     def wait(index, target, count):
         whole = target.at[pl.ds(0, count)]
@@ -123,25 +137,20 @@
         copy.wait_recv()
         copy.wait_send()
 
-    exchange(0, lambda peer: send1.at[lax.div(peer, dp_size)], recv1)
+    exchange(0, lambda to_expert, to_dp: send1.at[to_expert], recv1)
     wait(0, recv1, peers - 1)
-
-    chunk = min(CHUNK, peers)
-    lines = chunk * 2
 
     @pl.loop(0, peers // chunk)
     def _(index):
         block = recv1[pl.ds(index * chunk, chunk)].reshape(chunk * MSG, step)
         at = pl.ds(pl.multiple_of(index * lines, lines), lines)
         for q, (low, high) in enumerate(spans):
-            piece = dot(select(chunk, q), block[:, : high - low], (1, 0)).astype(BF16)
+            piece = dot(of_chunk[q], block[:, : high - low], (1, 0)).astype(BF16)
             x_ref[at, low:high] = piece[:lines]
             g_ref[at, low:high] = piece[lines:]
 
     loads[3].wait()
     loads[4].wait()
-    stores[0].start()
-    stores[1].start()
     rows, g_rows = x_ref[...], g_ref[...]
     pre = dot(rows, inner_ref[...], (1, 0))
     g_hidden = dot(g_rows, outer_ref[...], (1, 1))
@@ -153,19 +162,14 @@
     g_pre = (g_hidden * slope).astype(BF16)
     hidden_ref[...] = hidden
     gpre_ref[...] = g_pre
-    stores[2].start()
-    stores[3].start()
     out_part = dot(hidden, outer_ref[...], (1, 0)).astype(BF16)
     g_part = dot(g_pre, inner_ref[...], (1, 1)).astype(BF16)
     for index in range(peers // chunk):
         at = slice(index * lines, (index + 1) * lines)
         both = jnp.concatenate([out_part[at], g_part[at]], axis=0)
-        send2[index * chunk : (index + 1) * chunk] = pack(both, chunk).reshape(chunk, MSG, step)
+        send2[index * chunk : (index + 1) * chunk] = pack(both, chunk, of_chunk).reshape(chunk, MSG, step)
     recv2[pl.ds(me, 1)] = send2[pl.ds(me, 1)]
-    exchange(1, lambda peer: send2.at[peer], recv2)
-    wait(1, recv2, peers - 1)
-
-    block = recv2[...].reshape(peers * MSG, step)
+    exchange(1, lambda to_expert, to_dp: send2.at[to_expert * dp_size + to_dp], recv2)
     shape = (2 * columns, peers * MSG)
     row = lax.broadcasted_iota(jnp.int32, shape, 0)
     line = lax.broadcasted_iota(jnp.int32, shape, 1)
@@ -175,10 +179,15 @@
     wanted = second * 2 + (column & 1)
     base = (column >> 1) * per_expert
     inside = (line >= base) & (line < base + per_expert)
+    takes = [
+        (inside & ((line & (MSG - 1)) == wanted + q * ROWS)).astype(BF16) for q in range(PIECES)
+    ]
+    wait(1, recv2, peers - 1)
+    block = recv2[...].reshape(peers * MSG, step)
+
     sums = []
     for q, (low, high) in enumerate(spans):
-        take = (inside & ((line & (MSG - 1)) == wanted + q * ROWS)).astype(BF16)
-        sums.append(dot(take, block[:, : high - low], (1, 0)))
+        sums.append(dot(takes[q], block[:, : high - low], (1, 0)))
     total = jnp.concatenate(sums, axis=1)
     slot_out = total[:columns].astype(BF16)
     g_slot_in = total[columns:].astype(BF16)
@@ -198,11 +207,9 @@
         return jnp.concatenate([values[:, :half], values[:, half:]], axis=0).astype(BF16)
 
     def spread(index, target, own, axis, size):
-        @pl.loop(1, size)
-        def _(offset):
-            other = lax.rem(own + offset, size)
+        for offset in range(1, size):
             where = {"expert": expert, "dp": dp}
-            where[axis] = other
+            where[axis] = shifted(own, offset, size)
             pltpu.make_async_remote_copy(
                 src_ref=target.at[own], dst_ref=target.at[own], send_sem=send_sem.at[index],
                 recv_sem=recv_sem.at[index], device_id=where, device_id_type=MESH,
@@ -219,8 +226,6 @@
     left_ref[...] = jnp.concatenate([dispatch_exact, g_logits.astype(F32)], axis=0).astype(BF16)
     right_ref[:columns] = g_slot_in
     right_ref[columns:] = params_ref[...]
-    stores[4].start()
-    stores[5].start()
     wait(2, part_a, dp_size - 1)
     part_b[pl.ds(expert, 1)] = add(part_a, dp_size).astype(BF16)[None]
     spread(3, part_b, expert, "expert", experts)
@@ -228,24 +233,12 @@
     folded = add(part_b, experts)
     gparams_ref[:, :half] = folded[:columns]
     gparams_ref[:, half:] = folded[columns:]
-    stores[6].start()
-    for store in stores:
-        store.wait()
 
 
 def weight_kernel(
-    x_hbm, g_hbm, hidden_hbm, gpre_hbm, left_hbm, right_hbm, gparams_hbm,
-    gtok_hbm, gout_hbm, ginner_hbm, gouter_hbm,
     x_ref, g_ref, hidden_ref, gpre_ref, left_ref, right_ref, gparams_ref,
-    gtok_ref, ginner_ref, gouter_ref, load_sem, store_sem,
+    gtok_hbm, gout_hbm, ginner_hbm, gouter_hbm, gtok_ref, ginner_ref, gouter_ref, store_sem,
 ):
-    pairs = (
-        (x_hbm, x_ref), (gpre_hbm, gpre_ref), (hidden_hbm, hidden_ref), (g_hbm, g_ref),
-        (left_hbm, left_ref), (right_hbm, right_ref), (gparams_hbm, gparams_ref),
-    )
-    loads = [pltpu.make_async_copy(a, b, load_sem.at[i]) for i, (a, b) in enumerate(pairs)]
-    for load in loads:
-        load.start()
     stores = []
 
     def product(left, right, out_ref, out_hbm):
@@ -257,16 +250,9 @@
             ))
             stores[-1].start()
 
-    loads[0].wait()
-    loads[1].wait()
     product(x_ref, gpre_ref, ginner_ref, ginner_hbm)
-    loads[2].wait()
-    loads[3].wait()
     product(hidden_ref, g_ref, gouter_ref, gouter_hbm)
-    loads[4].wait()
-    loads[5].wait()
     product(left_ref, right_ref, gtok_ref, gtok_hbm)
-    loads[6].wait()
     stores.append(pltpu.make_async_copy(gparams_ref, gout_hbm, store_sem.at[len(stores)]))
     stores[-1].start()
     for store in stores:
@@ -283,7 +269,8 @@
     units = inner_weight.shape[2]
     rows = peers * 2
     step, _ = pieces_of(width)
-    hbm = pl.BlockSpec(memory_space=pl.ANY)
+    hbm = pl.BlockSpec(memory_space=pltpu.HBM)
+    vmem = pl.BlockSpec(memory_space=pltpu.VMEM)
     shape = jax.ShapeDtypeStruct
     small = (
         shape((rows, width), BF16),
@@ -294,13 +281,12 @@
         shape((2 * columns, width), BF16),
         shape((columns, width), F32),
     )
-    held = [pltpu.VMEM(s.shape, s.dtype) for s in small]
     small = pl.pallas_call(
         functools.partial(kernel, experts, dp_size),
         out_shape=small,
         in_specs=[hbm] * 5,
-        out_specs=[hbm] * 7,
-        scratch_shapes=held + [
+        out_specs=[vmem] * 7,
+        scratch_shapes=[
             pltpu.VMEM((patches, width), BF16),
             pltpu.VMEM((patches, width), BF16),
             pltpu.VMEM((columns, width), BF16),
@@ -313,7 +299,6 @@
             pltpu.VMEM((dp_size, 2 * columns, width // 2), BF16),
             pltpu.VMEM((experts, 2 * columns, width // 2), BF16),
             pltpu.SemaphoreType.DMA((5,)),
-            pltpu.SemaphoreType.DMA((7,)),
             pltpu.SemaphoreType.DMA((4,)),
             pltpu.SemaphoreType.DMA((4,)),
         ],
@@ -331,13 +316,12 @@
     g_tokens, g_params, grad_inner, grad_outer = pl.pallas_call(
         weight_kernel,
         out_shape=results,
-        in_specs=[hbm] * 7,
+        in_specs=[vmem] * 7,
         out_specs=[hbm] * 4,
-        scratch_shapes=held + [
+        scratch_shapes=[
             pltpu.VMEM((patches, width), BF16),
             pltpu.VMEM((width, units), BF16),
             pltpu.VMEM((units, width), BF16),
-            pltpu.SemaphoreType.DMA((7,)),
             pltpu.SemaphoreType.DMA((store_count,)),
         ],
         compiler_params=pltpu.CompilerParams(vmem_limit_bytes=VMEM_BYTES),

time: 34.7 us -> 33.8 us (0.974)
  Pallas kernels: 33.9 us -> 32.3 us
  local copies, waits for them, and re-layouts: 0 us -> 0.72 us
    pallas_call x1, Pallas kernels: 4.08 us -> 3 us  [local(): pl.pallas_call(weight_kernel, out_shape=results, in_specs=[vmem] * 7, out...]
    unnamed x0 -> x2, local copies, waits for them, and re-layouts: none -> 0.72 us
    pallas_call x1, Pallas kernels: 29.8 us -> 29.3 us  [local(): pl.pallas_call(functools.partial(kernel, experts, dp_size), out_shape=sma...]
where the time goes in v3:
time: 33.8 us; the launch traced here: 33.7 us
  Pallas kernels  32.3 us (96%)
  local copies, waits for them, and re-layouts  0.72 us (2%)
  between operations  0.65 us (2%)
    pallas_call x1, Pallas kernels, local(): pl.pallas_call(functools.partial(kernel, experts, dp_size), out_shape=sma...  29.3 us
    pallas_call x1, Pallas kernels, local(): pl.pallas_call(weight_kernel, out_shape=results, in_specs=[vmem] * 7, out...  3 us
    unnamed x2, local copies, waits for them, and re-layouts  0.72 us

profile of v3, /device:TPU:0, one launch (start us, length us, event | category | flops | bytes accessed | tf_op | source)
XLA Modules:
  0.0 33.7 jit_solution(16851159147223713312)
XLA Ops:
  0.6 0.0 copy-start
  0.6 0.7 %copy-done = bf16[1280,8]{0,1:T(8,128)(2,1)S(1)} copy-done((bf16[1280,8]{0,1:T(8,128)(2,1)S(1)}, bf16[1280,8]{0,1:T(8,128)(2,1)}, u32[]{:S(2)}) %copy-start) | copy-done | bytes 20504
  1.4 29.3 %shard_map.84 = (bf16[32,1280]{1,0:T(8,128)(2,1)S(1)}, bf16[32,1280]{1,0:T(8,128)(2,1)S(1)}, bf16[32,1024]{1,0:T(8,128)(2,1)S(1)}, bf16[32,1024]{1,0:T(8,128)(2,...) custom-call(bf16[256,1280]{1,0:T(8,128)(2,1)} %bitcast.12, ...), custom_call_target="tpu_custom_call" | custom-call | tf_op jit(solution)/shard_map/pallas_call | solution.py:284
  30.7 3.0 %shard_map.85 = (bf16[256,1280]{1,0:T(8,128)(2,1)}, f32[8,1280]{1,0:T(8,128)}, bf16[1280,1024]{1,0:T(8,128)(2,1)}, bf16[1024,1280]{1,0:T(8,128)(2,1)}) custom-call(bf16[32,1280]{1,0:T(8,128)(2,1)S(1)} %get-tuple-element.15.x_ref, bf16[32,1280]{1,0:T(8,128)(2,1)S(1)} %get-tuple-element.16.g_ref, bf16[32,1024]{1,0:T(8,128)(2,1)S(1)} %get-tuple-element.17.hidden_ref, ...), custom_call_target="tpu_custom_call" | custom-call | tf_op jit(solution)/shard_map/pallas_call | solution.py:316
Async XLA Ops:
  0.6 0.7 %copy-start = (bf16[1280,8]{0,1:T(8,128)(2,1)S(1)}, bf16[1280,8]{0,1:T(8,128)(2,1)}, u32[]{:S(2)}) copy-start(bf16[1280,8]{0,1:T(8,128)(2,1)} %param.7) | copy-start | bytes 61444

commit v4 on v3

--- a/solution.py
+++ b/solution.py
@@ -76,8 +76,8 @@
 
     def every_peer(body):
         if peers <= CHUNK:
-            for across in range(experts):
-                for along in range(dp_size):
+            for along in reversed(range(dp_size)):
+                for across in reversed(range(experts)):
                     if across or along:
                         body(shifted(expert, across, experts), shifted(dp, along, dp_size))
         else:

time: 33.8 us -> 32.3 us (0.956)
  Pallas kernels: 32.3 us -> 30.8 us
    pallas_call x1, Pallas kernels: 29.3 us -> 27.8 us  [local(): pl.pallas_call(functools.partial(kernel, experts, dp_size), out_shape=sma...]
where the time goes in v4:
time: 32.3 us; the launch traced here: 32.1 us
  Pallas kernels  30.8 us (95%)
  local copies, waits for them, and re-layouts  0.72 us (2%)
  between operations  0.65 us (2%)
    pallas_call x1, Pallas kernels, local(): pl.pallas_call(functools.partial(kernel, experts, dp_size), out_shape=sma...  27.8 us
    pallas_call x1, Pallas kernels, local(): pl.pallas_call(weight_kernel, out_shape=results, in_specs=[vmem] * 7, out...  3 us
    unnamed x2, local copies, waits for them, and re-layouts  0.72 us

profile of v4, /device:TPU:0, one launch (start us, length us, event | category | flops | bytes accessed | tf_op | source)
XLA Modules:
  0.0 32.1 jit_solution(9792311959575819544)
XLA Ops:
  0.6 0.0 copy-start
  0.6 0.7 %copy-done = bf16[1280,8]{0,1:T(8,128)(2,1)S(1)} copy-done((bf16[1280,8]{0,1:T(8,128)(2,1)S(1)}, bf16[1280,8]{0,1:T(8,128)(2,1)}, u32[]{:S(2)}) %copy-start) | copy-done | bytes 20504
  1.4 27.8 %shard_map.84 = (bf16[32,1280]{1,0:T(8,128)(2,1)S(1)}, bf16[32,1280]{1,0:T(8,128)(2,1)S(1)}, bf16[32,1024]{1,0:T(8,128)(2,1)S(1)}, bf16[32,1024]{1,0:T(8,128)(2,...) custom-call(bf16[256,1280]{1,0:T(8,128)(2,1)} %bitcast.12, ...), custom_call_target="tpu_custom_call" | custom-call | tf_op jit(solution)/shard_map/pallas_call | solution.py:284
  29.1 3.0 %shard_map.85 = (bf16[256,1280]{1,0:T(8,128)(2,1)}, f32[8,1280]{1,0:T(8,128)}, bf16[1280,1024]{1,0:T(8,128)(2,1)}, bf16[1024,1280]{1,0:T(8,128)(2,1)}) custom-call(bf16[32,1280]{1,0:T(8,128)(2,1)S(1)} %get-tuple-element.15.x_ref, bf16[32,1280]{1,0:T(8,128)(2,1)S(1)} %get-tuple-element.16.g_ref, bf16[32,1024]{1,0:T(8,128)(2,1)S(1)} %get-tuple-element.17.hidden_ref, ...), custom_call_target="tpu_custom_call" | custom-call | tf_op jit(solution)/shard_map/pallas_call | solution.py:316
Async XLA Ops:
  0.6 0.7 %copy-start = (bf16[1280,8]{0,1:T(8,128)(2,1)S(1)}, bf16[1280,8]{0,1:T(8,128)(2,1)}, u32[]{:S(2)}) copy-start(bf16[1280,8]{0,1:T(8,128)(2,1)} %param.7) | copy-start | bytes 61444
